TPU v7x, 128 devices: a whole 4x4x4 slice. The times are simulated.
128 devices in a mesh: row: 8 (over x_lo, z), col: 4 (over x_hi, core), rep: 4 (over y).
Axes of the slice: x: 4 (x_hi: 2, x_lo: 2; x = x_hi * 2 + x_lo), y: 4, z: 4, core: 2. Of those that a mesh axis runs over, the one named last changes fastest.
Arguments:
- p_matrix: bfloat16 [49152, 16384], P('row', ('col', 'rep')), may hold values from -6 to 6
- s_matrix: bfloat16 [16384, 2048], P(('col', 'rep')), may hold values from -0.09375 to 0.09375
- p_pattern: int32 [384, 128], P('row', ('col', 'rep')), may hold values 0 or 1
- s_pattern: int32 [128, 16], P(('col', 'rep')), may hold values 0 or 1
- c_input: float32 [49152, 2048], P('row', ('col', 'rep')), may hold values from -6 to 6
- step: int32 [1], replicated, may hold values from 0 to 4095
Outputs:
- c_output: float32 [49152, 2048], P('row', ('col', 'rep'))
All inputs are finite; a program needn't handle non-finite values. No bound on the sum of `p_pattern` or of `s_pattern` on one device may be relied on, other than what follows from the above.
Results may differ from a plain program's by a relative error of at most 0.005.
Values may be sent and summed in bfloat16 or wider, within the bound.
A program may use at most 128 MiB of HBM per device.

v0:
```python
import jax
import jax.numpy as jnp
from jax import lax
from jax.sharding import PartitionSpec as P

BLOCK = 128


def from_behind(value, axis, steps):
    count = lax.axis_size(axis)
    pairs = [(source, (source + steps) % count) for source in range(count)]
    return lax.ppermute(value, axis, pairs)


def masked(matrix, pattern):
    row_blocks, col_blocks = pattern.shape
    shaped = matrix.reshape(row_blocks, BLOCK, col_blocks, BLOCK)
    shaped = shaped * pattern[:, None, :, None].astype(matrix.dtype)
    return shaped.reshape(row_blocks * BLOCK, col_blocks * BLOCK)


def local(p_matrix, s_matrix, p_pattern, s_pattern, c_input, step):
    col_count = lax.axis_size("col")
    col_index = lax.axis_index("col")
    distance = (lax.axis_index("row") + step[0]) % col_count
    p_panel = masked(p_matrix, p_pattern)
    s_slab = masked(s_matrix, s_pattern)
    col_group = s_slab.shape[1] // col_count
    for bit_number in range(col_count.bit_length() - 1):
        arrived = from_behind((p_panel, s_slab), "col", col_count - (1 << bit_number))
        take_it = (distance >> bit_number) % 2 == 1
        p_panel = jnp.where(take_it, arrived[0], p_panel)
        s_slab = jnp.where(take_it, arrived[1], s_slab)
    s_slab = lax.dynamic_slice_in_dim(s_slab, col_index * col_group, col_group, 1)
    partial_value = jnp.dot(p_panel, s_slab, preferred_element_type=jnp.float32)
    summed = lax.psum_scatter(
        partial_value.astype(jnp.bfloat16), "rep", scatter_dimension=1, tiled=True
    ).astype(jnp.float32)
    return c_input + summed


def solution(mesh):
    placed = (
        P("row", ("col", "rep")),
        P(("col", "rep"), None),
        P("row", ("col", "rep")),
        P(("col", "rep"), None),
        P("row", ("col", "rep")),
        P(),
    )
    return jax.shard_map(
        local, mesh=mesh, in_specs=placed, out_specs=P("row", ("col", "rep")), check_vma=False
    )
```

profile of v0, /device:TPU:1, one launch (start us, length us, event | category | flops | bytes accessed | tf_op | source)
XLA Modules:
  0.0 693.2 jit_solution(8894082251685761167)
XLA Ops:
  6.5 0.0 reduce-scatter.4.cloned.1.call-start
  6.5 0.7 convert_element_type.14
  7.2 0.1 copy.8
  7.3 6.2 mul.25
  13.5 14.0 %bitcast_multiply_fusion = bf16[6144,1024]{1,0:T(8,128)(2,1)} fusion(bf16[6144,1024]{1,0:T(8,128)(2,1)} %param.6, bf16[768,8,8,128]{3,2,1,0:T(8,128)(2,1)} %bitcast.12), kind=kLoop, calls=%fused_computation | loop fusion | flops 6291456 | bytes 37748736 | tf_op jit(solution)/shard_map/mul | solution.py:18
  27.6 1.4 collective-permute-start
  29.7 0.0 copy-start.1
  29.7 138.4 %collective-permute-done = bf16[6144,1024]{1,0:T(8,128)(2,1)} collective-permute-done((bf16[6144,1024]{1,0:T(8,128)(2,1)}, bf16[6144,1024]{1,0:T(8,128)(2,1)}, u32[]{:S(2)}, u32[]{:S(2)}) %collective-permute-start) | collective-permute-done | bytes 12582944 | tf_op jit(solution)/shard_map/ppermute | solution.py:12
  168.1 10.6 %broadcast_select_fusion = bf16[6144,1024]{1,0:T(8,128)(2,1)} fusion(bf16[6144,1024]{1,0:T(8,128)(2,1)} %collective-permute-done, bf16[6144,1024]{1,0:T(8,128)(2,1)} %bitcast_multiply_fusion, pred[]{:T(512)S(6)} %eq.11), kind=kLoop, calls=%fused_computation.3 | loop fusion | flops 6291456 | bytes 37748736 | tf_op jit(solution)/shard_map/jit(_where)/select_n | solution.py:32
  178.7 0.0 copy-start
  178.7 2.7 collective-permute-start.1
  181.4 0.0 copy-done.1
  181.4 0.6 mul.28
  182.0 0.0 copy-done
  182.1 0.9 bitcast_multiply_fusion.1
  183.0 0.1 collective-permute-start.2
  183.1 314.4 %collective-permute-done.2 = bf16[1024,2048]{1,0:T(8,128)(2,1)S(1)} collective-permute-done((bf16[1024,2048]{1,0:T(8,128)(2,1)S(1)}, bf16[1024,2048]{1,0:T(8,128)(2,1)S(1)}, u32[]{:S(2)}, u32[]{:S(2)}) %collective-permute-start.2) | collective-permute-done | bytes 4194336 | tf_op jit(solution)/shard_map/ppermute | solution.py:12
  497.5 2.4 broadcast_select_fusion.1
  499.9 0.4 collective-permute-start.3
  500.3 91.6 %collective-permute-done.3 = bf16[1024,2048]{1,0:T(8,128)(2,1)} collective-permute-done((bf16[1024,2048]{1,0:T(8,128)(2,1)}, bf16[1024,2048]{1,0:T(8,128)(2,1)}, u32[]{:S(2)}, u32[]{:S(2)}) %collective-permute-start.3) | collective-permute-done | bytes 4194336 | tf_op jit(solution)/shard_map/ppermute | solution.py:12
  591.8 0.0 collective-permute-done.1
  591.8 13.6 %fusion.3 = bf16[6144,512]{1,0:T(8,128)(2,1)} fusion(bf16[6144,1024]{1,0:T(8,128)(2,1)} %collective-permute-done.1, bf16[6144,1024]{1,0:T(8,128)(2,1)} %broadcast_select_fusion, pred[]{:T(512)S(6)} %eq.10, bf16[1024,2048]{1,0:T(8,128)(2,1)} %broadcast_select_fusion.1, s32[]{:T(128)S(6)} %select_n.57, bf16[1024,2048]{1,0:T(8,128)(2,1)} %collective-permute-done.3), kind=kOutput, calls=%fused_computation.5 | convolution fusion | flops 6452412416 | bytes 33555968 | tf_op jit(solution)/shard_map/dot_general | solution.py:35
  605.5 8.7 %copy.9 = bf16[6144,512]{0,1:T(8,128)(2,1)} copy(bf16[6144,512]{1,0:T(8,128)(2,1)} %fusion.3) | data formatting | bytes 12582912
  614.2 0.0 reduce-scatter.4.cloned.1.call-update
  614.2 66.4 %reduce-scatter.4.cloned.1.call-done = bf16[128,6144]{1,0:T(8,128)(2,1)} async-done(((bf16[512,6144]{1,0:T(8,128)(2,1)}), bf16[128,6144]{1,0:T(8,128)(2,1)}) %reduce-scatter.4.cloned.1.call-update) | async-done | bytes 1572880
  680.6 1.9 copy.10
  682.5 3.8 convert_add_fusion
  (1 shorter events, 0.0 us)
Async XLA Ops:
  6.5 674.1 %reduce-scatter.4.cloned.1.call-start = ((), (), s32[]{:S(2)}) async-start(), calls=%async_computation.1 | async-start | bytes 7864320
  27.6 140.5 %collective-permute-start = (bf16[6144,1024]{1,0:T(8,128)(2,1)}, bf16[6144,1024]{1,0:T(8,128)(2,1)}, u32[]{:S(2)}, u32[]{:S(2)}) collective-permute-start(bf16[6144,1024]{1,0:T(8,128)(2,1)} %bitcast_multiply_fusion), channel_id=1, source_target_pairs={{0,12},{4,0},{8,4},{12,8},{1,13},{5,1},{9,5},{13,9},{2,14},{6,2},{... | collective-permute-start | bytes 37748744 | tf_op jit(solution)/shard_map/ppermute | solution.py:12
  29.7 151.7 %copy-start.1 = (s32[8,16]{1,0:T(8,128)S(1)}, s32[8,16]{1,0:T(8,128)}, u32[]{:S(2)}) copy-start(s32[8,16]{1,0:T(8,128)} %param.9) | copy-start | bytes 1540
  178.7 3.3 copy-start
  178.7 413.1 %collective-permute-start.1 = (bf16[6144,1024]{1,0:T(8,128)(2,1)}, bf16[6144,1024]{1,0:T(8,128)(2,1)}, u32[]{:S(2)}, u32[]{:S(2)}) collective-permute-start(bf16[6144,1024]{1,0:T(8,128)(2,1)} %broadcast_select_fusion), channel_id=1, source_target_pairs={{0,8},{4,12},{8,0},{12,4},{1,9},{5,13},{9,1},{13,5},{2,10},{6,14},... | collective-permute-start | bytes 37748744 | tf_op jit(solution)/shard_map/ppermute | solution.py:12
  183.0 314.5 %collective-permute-start.2 = (bf16[1024,2048]{1,0:T(8,128)(2,1)S(1)}, bf16[1024,2048]{1,0:T(8,128)(2,1)S(1)}, u32[]{:S(2)}, u32[]{:S(2)}) collective-permute-start(bf16[1024,2048]{1,0:T(8,128)(2,1)S(1)} %bitcast_multiply_fusion.1), channel_id=1, source_target_pairs={{0,12},{4,0},{8,4},{12,8},{1,13},{5,1},{9,5},{13,9},{2,14},{6,2},{... | collective-permute-start | bytes 12582920 | tf_op jit(solution)/shard_map/ppermute | solution.py:12
  499.9 92.0 %collective-permute-start.3 = (bf16[1024,2048]{1,0:T(8,128)(2,1)}, bf16[1024,2048]{1,0:T(8,128)(2,1)}, u32[]{:S(2)}, u32[]{:S(2)}) collective-permute-start(bf16[1024,2048]{1,0:T(8,128)(2,1)} %broadcast_select_fusion.1), channel_id=1, source_target_pairs={{0,8},{4,12},{8,0},{12,4},{1,9},{5,13},{9,1},{13,5},{2,10},{6,14},... | collective-permute-start | bytes 12582920 | tf_op jit(solution)/shard_map/ppermute | solution.py:12
Sparse Core Ops, SparseCore 0:
  614.3 66.2 reduce-scatter.3
where the time goes:
time: 694 us; the launch traced here: 693 us
  waiting for transfers between devices  611 us (88%)
  other arithmetic  32.5 us (5%)
  local copies, waits for them, and re-layouts  17.5 us (3%)
  between operations  14.1 us (2%)
  matrix products  13.6 us (2%)
    ppermute x4, waiting for transfers between devices, from_behind(): return lax.ppermute(value, axis, pairs)  544 us
    unnamed x2, waiting for transfers between devices  66.4 us
    mul x2, other arithmetic, masked(): shaped = shaped * pattern[:, None, :, None].astype(matrix.dtype)  14.9 us
  transfers between devices with their start and end apart: 5, of which 4 were waited for; matrix products, arithmetic and copies ran while one was open for 1% of the time, Pallas kernels for 0%

commit v1 on v0

v1 whole, which is shorter than its diff:
```python
import functools

import jax
import jax.numpy as jnp
from jax import lax
from jax.experimental import pallas as pl
from jax.experimental.pallas import tpu as pltpu
from jax.sharding import PartitionSpec as P

BLOCK = 128
CHUNK = 512
HALF = CHUNK // 2
LAG_ADD, LAG_SUM, LAG_OUT = 2, 4, 6
MESH = pl.DeviceIdType.MESH


def kernel(
    shift, chunks, p_pat, s_pat, p_hbm, s_hbm, c_hbm, o_hbm,
    p_v, s_v, c_v, o_v, own, wait_lo, wait_hi, far_s, lo_s, hi_s, move_s,
    far_r, lo_r, hi_r, move_r,
    p_sem, s_sem, c_sem, o_sem, far_ss, far_rs, lo_ss, lo_rs, hi_ss, hi_rs, move_ss, move_rs,
):
    row, col, rep = lax.axis_index("row"), lax.axis_index("col"), lax.axis_index("rep")
    distance = lax.rem(row + shift, 4)
    target = lax.rem(col + 4 - distance, 4)
    origin = lax.rem(col + distance, 4)
    group = target
    up, down = {"rep": lax.rem(rep + 1, 4)}, {"rep": lax.rem(rep + 3, 4)}
    moves = distance != 0

    barrier = pltpu.get_barrier_semaphore()
    for neighbour in (up, down):
        pl.semaphore_signal(barrier, inc=1, device_id=neighbour, device_id_type=MESH)

    @pl.when(moves)
    def _():
        pl.semaphore_signal(barrier, inc=1, device_id={"col": target}, device_id_type=MESH)
        pl.semaphore_signal(barrier, inc=1, device_id={"col": origin}, device_id_type=MESH)

    def s_load(k):
        at = pl.multiple_of((group * 4 + lax.rem(rep + k, 4)) * BLOCK, BLOCK)
        return pltpu.make_async_copy(
            s_hbm.at[:, pl.ds(at, BLOCK)], s_v.at[:, pl.ds(k * BLOCK, BLOCK)], s_sem.at[k]
        )

    def p_load(i):
        return pltpu.make_async_copy(p_hbm.at[pl.ds(i * CHUNK, CHUNK)], p_v.at[i], p_sem.at[i])

    def c_load():
        return pltpu.make_async_copy(c_hbm, c_v, c_sem)

    def o_store(i):
        return pltpu.make_async_copy(o_v.at[i], o_hbm.at[pl.ds(i * CHUNK, CHUNK)], o_sem.at[i])

    def remote(source, target_ref, send, receive, device):
        return pltpu.make_async_remote_copy(
            src_ref=source, dst_ref=target_ref, send_sem=send, recv_sem=receive,
            device_id=device, device_id_type=MESH,
        )

    def far_down(i):
        return remote(far_s.at[i, 0], far_r.at[i, 0], far_ss.at[i, 0], far_rs.at[i, 0], down)

    def far_up(i):
        return remote(far_s.at[i, 1], far_r.at[i, 1], far_ss.at[i, 1], far_rs.at[i, 1], up)

    def near_down(i):
        return remote(lo_s.at[i], hi_r.at[i], lo_ss.at[i], hi_rs.at[i], down)

    def near_up(i):
        return remote(hi_s.at[i], lo_r.at[i], hi_ss.at[i], lo_rs.at[i], up)

    def move(i):
        return remote(move_s.at[i], move_r.at[i], move_ss.at[i], move_rs.at[i], {"col": target})

    for k in range(4):
        s_load(k).start()
    p_load(0).start()
    p_load(1).start()
    c_load().start()

    def start_p(i, carry):
        p_load(i).start()
        return carry

    lax.fori_loop(2, chunks, start_p, 0)

    for k in range(4):
        s_load(k).wait()
        for b in range(8):
            rows, columns = pl.ds(b * BLOCK, BLOCK), pl.ds(k * BLOCK, BLOCK)
            keep = s_pat[b, group * 4 + lax.rem(rep + k, 4)].astype(jnp.float32).astype(jnp.bfloat16)
            s_v[rows, columns] = s_v[rows, columns] * keep

    def produce(i):
        p_load(i).wait()
        for a in range(CHUNK // BLOCK):
            for b in range(8):
                rows, columns = pl.ds(a * BLOCK, BLOCK), pl.ds(b * BLOCK, BLOCK)
                keep = p_pat[i * (CHUNK // BLOCK) + a, b].astype(jnp.float32).astype(jnp.bfloat16)
                p_v[i, rows, columns] = p_v[i, rows, columns] * keep
        term = jnp.dot(p_v[i], s_v[...], preferred_element_type=jnp.float32)
        far = term[:, 2 * BLOCK:3 * BLOCK].astype(jnp.bfloat16)
        far_s[i, 0] = far[:HALF]
        far_s[i, 1] = far[HALF:]
        own[i] = term[:, :BLOCK]
        hi_s[i, :HALF] = term[:HALF, BLOCK:2 * BLOCK].astype(jnp.bfloat16)
        wait_hi[i] = term[HALF:, BLOCK:2 * BLOCK]
        wait_lo[i] = term[:HALF, 3 * BLOCK:]
        lo_s[i, HALF:] = term[HALF:, 3 * BLOCK:].astype(jnp.bfloat16)

    def send_far(i):
        far_down(i).start()
        far_up(i).start()

    def add(i):
        far_down(i).wait_recv()
        lo_s[i, :HALF] = (wait_lo[i] + far_r[i, 0].astype(jnp.float32)).astype(jnp.bfloat16)
        near_down(i).start()
        far_up(i).wait_recv()
        hi_s[i, HALF:] = (wait_hi[i] + far_r[i, 1].astype(jnp.float32)).astype(jnp.bfloat16)
        near_up(i).start()

    def total(i):
        near_down(i).wait_recv()
        near_up(i).wait_recv()
        summed = own[i] + hi_r[i].astype(jnp.float32) + lo_r[i].astype(jnp.float32)
        summed = summed.astype(jnp.bfloat16)

        @pl.when(moves)
        def _():
            move_s[i] = summed
            move(i).start()

        @pl.when(jnp.logical_not(moves))
        def _():
            move_r[i] = summed

    def finish(i):
        @pl.when(moves)
        def _():
            move(i).wait_recv()

        at = pl.ds(i * CHUNK, CHUNK)
        o_v[i] = c_v[at] + move_r[i].astype(jnp.float32)
        o_store(i).start()

    produce(0)

    @pl.when(moves)
    def _():
        pl.semaphore_wait(barrier, 4)

    @pl.when(jnp.logical_not(moves))
    def _():
        pl.semaphore_wait(barrier, 2)

    send_far(0)
    c_load().wait()

    def body(t, carry):
        @pl.when(t < chunks)
        def _():
            produce(t)
            send_far(t)

        @pl.when(jnp.logical_and(t >= LAG_ADD, t < chunks + LAG_ADD))
        def _():
            add(t - LAG_ADD)

        @pl.when(jnp.logical_and(t >= LAG_SUM, t < chunks + LAG_SUM))
        def _():
            total(t - LAG_SUM)

        @pl.when(t >= LAG_OUT)
        def _():
            finish(t - LAG_OUT)

        return carry

    lax.fori_loop(1, chunks + LAG_OUT, body, 0)

    def drain(i, carry):
        far_down(i).wait_send()
        far_up(i).wait_send()
        near_down(i).wait_send()
        near_up(i).wait_send()

        @pl.when(moves)
        def _():
            move(i).wait_send()

        o_store(i).wait()
        return carry

    lax.fori_loop(0, chunks, drain, 0)


def cannon_step(shift, p_matrix, s_matrix, p_pattern, s_pattern, c_input):
    rows, depth = p_matrix.shape
    chunks = rows // CHUNK
    width = c_input.shape[1]
    dma = pltpu.SemaphoreType.DMA
    half = lambda dtype, *lead: pltpu.VMEM((chunks, *lead, HALF, width), dtype)
    full = lambda dtype: pltpu.VMEM((chunks, CHUNK, width), dtype)
    return pl.pallas_call(
        functools.partial(kernel, shift, chunks),
        out_shape=jax.ShapeDtypeStruct(c_input.shape, jnp.float32),
        in_specs=[pl.BlockSpec(memory_space=pltpu.SMEM)] * 2 + [pl.BlockSpec(memory_space=pl.ANY)] * 3,
        out_specs=pl.BlockSpec(memory_space=pl.ANY),
        scratch_shapes=[
            pltpu.VMEM((chunks, CHUNK, depth), jnp.bfloat16),
            pltpu.VMEM((depth, 4 * width), jnp.bfloat16),
            pltpu.VMEM((rows, width), jnp.float32),
            full(jnp.float32),
            full(jnp.float32),
            half(jnp.float32), half(jnp.float32),
            half(jnp.bfloat16, 2),
            full(jnp.bfloat16), full(jnp.bfloat16), full(jnp.bfloat16),
            half(jnp.bfloat16, 2),
            full(jnp.bfloat16), full(jnp.bfloat16), full(jnp.bfloat16),
            dma((chunks,)), dma((4,)), dma, dma((chunks,)),
            dma((chunks, 2)), dma((chunks, 2)),
            dma((chunks,)), dma((chunks,)), dma((chunks,)), dma((chunks,)),
            dma((chunks,)), dma((chunks,)),
        ],
        compiler_params=pltpu.CompilerParams(
            collective_id=shift, has_side_effects=True, vmem_limit_bytes=56 * 2**20
        ),
        cost_estimate=pl.CostEstimate(
            flops=2 * rows * depth * 4 * width, bytes_accessed=20 * 2**20, transcendentals=0
        ),
    )(p_pattern, s_pattern, p_matrix, s_matrix, c_input)


def local(p_matrix, s_matrix, p_pattern, s_pattern, c_input, step):
    return lax.switch(
        lax.rem(step[0], 4),
        [functools.partial(cannon_step, shift) for shift in range(4)],
        p_matrix, s_matrix, p_pattern, s_pattern, c_input,
    )


def solution(mesh):
    placed = (
        P("row", ("col", "rep")),
        P(("col", "rep"), None),
        P("row", ("col", "rep")),
        P(("col", "rep"), None),
        P("row", ("col", "rep")),
        P(),
    )
    return jax.shard_map(
        local, mesh=mesh, in_specs=placed, out_specs=P("row", ("col", "rep")), check_vma=False
    )
```

time: 694 us -> 70 us (0.10)
  the two profiles are of different devices: /device:TPU:1 before, /device:TPU:96 now
where the time goes in v1:
time: 70 us; the launch traced here: 69.8 us
  Pallas kernels  66 us (94%)
  local copies, waits for them, and re-layouts  3.04 us (4%)
    pallas_call x1, Pallas kernels, cannon_step(): pl.pallas_call(functools.partial(kernel, shift, chunks), out_shape=jax.Sh...  66 us
    unnamed x1, local copies, waits for them, and re-layouts  1.67 us

profile of v1, /device:TPU:96, one launch (start us, length us, event | category | flops | bytes accessed | tf_op | source)
XLA Modules:
  0.0 69.8 jit_solution(14510391574133490755)
XLA Ops:
  0.7 67.4 %conditional.1 = (f32[6144,128]{1,0:T(8,128)S(1)}) conditional(s32[]{:T(128)} %clamp.3, (s32[48,8]{0,1:T(8,128)}, s32[8,16]{1,0:T(8,128)}, bf16[6144,1024]{1,0:T(8,128)(2,1)}, bf16[1024,2048]{1,0:T(8,128)(2,1)}, f32[6144,128]{1,0:T(8,128)}) %tuple.17, (s32[48,8]{0,1:T(8,128)}, s32[8,16]{1,0:T(8,128)}, ...), branch_computations={%region_0.0_spmd, %region_1.0_spmd, %region_2.0_spmd, %region_3.0_... | conditional | flops 6442450944 | bytes 20974600 | solution.py:237
  0.7 1.4 %copy.14.p_pat = s32[48,8]{1,0:T(8,128)} copy(s32[48,8]{0,1:T(8,128)} %get-tuple-element.86) | data formatting | bytes 3072 | tf_op jit(solution)/shard_map
  2.1 66.0 %branch_3_fun.1 = f32[6144,128]{1,0:T(8,128)S(1)} custom-call(s32[48,8]{1,0:T(8,128)} %copy.14.p_pat, s32[8,16]{1,0:T(8,128)} %get-tuple-element.66.s_pat, bf16[6144,1024]{1,0:T(8,128)(2,1)} %get-tuple-element.67.p_hbm, bf16[1024,2048]{1,0:T(8,128)(2,1)} %get-tuple-element.68.s_hbm, f32[6144,128]{1,0:T(8,128)} %get-tuple-element.69.c_hbm), custom_call_target="tpu_custom_call" | custom-call | flops 6442450944 | bytes 20971520 | tf_op jit(solution)/shard_map/cond/branch_3_fun/pallas_call | solution.py:206
  68.1 1.7 %copy.21 = f32[6144,128]{1,0:T(8,128)} copy(f32[6144,128]{1,0:T(8,128)S(1)} %get-tuple-element.70) | data formatting | bytes 6291456

commit v2 on v1

v2 whole, which is shorter than its diff:
```python
import functools

import jax
import jax.numpy as jnp
from jax import lax
from jax.experimental import pallas as pl
from jax.experimental.pallas import tpu as pltpu
from jax.sharding import PartitionSpec as P

BLOCK = 128
CHUNK = 512
HALF = CHUNK // 2
EARLY = 2
AHEAD = 2
LAG_ADD, LAG_SUM, LAG_OUT = 2, 4, 6
MESH = pl.DeviceIdType.MESH


def kernel(
    shift, chunks, pp_hbm, sp_hbm, p_hbm, s_hbm, c_hbm, o_hbm,
    p_pat, s_pat, p_v, s_v, c_v, o_v, own, wait_lo, wait_hi, far_s, lo_s, hi_s, move_s, mid_s,
    far_r, lo_r, hi_r, move_r, mid_r,
    pat_sem, p_sem, s_sem, c_sem, o_sem, far_ss, far_rs, lo_ss, lo_rs, hi_ss, hi_rs,
    move_ss, move_rs, mid_ss, mid_rs,
):
    row, col, rep = lax.axis_index("row"), lax.axis_index("col"), lax.axis_index("rep")
    distance = lax.rem(row + shift, 4)
    target = lax.rem(col + 4 - distance, 4)
    origin = lax.rem(col + distance, 4)
    group = target
    up, down, across = {"rep": lax.rem(rep + 1, 4)}, {"rep": lax.rem(rep + 3, 4)}, {"col": target}
    moves = distance != 0
    stays = distance == 0

    barrier = pltpu.get_barrier_semaphore()
    for neighbour in (up, down):
        pl.semaphore_signal(barrier, inc=1, device_id=neighbour, device_id_type=MESH)

    @pl.when(moves)
    def _():
        pl.semaphore_signal(barrier, inc=1, device_id=across, device_id_type=MESH)
        pl.semaphore_signal(barrier, inc=1, device_id={"col": origin}, device_id_type=MESH)

    def s_load(k):
        at = pl.multiple_of((group * 4 + lax.rem(rep + k, 4)) * BLOCK, BLOCK)
        return pltpu.make_async_copy(
            s_hbm.at[:, pl.ds(at, BLOCK)], s_v.at[:, pl.ds(k * BLOCK, BLOCK)], s_sem.at[k]
        )

    def p_load(i):
        return pltpu.make_async_copy(p_hbm.at[pl.ds(i * CHUNK, CHUNK)], p_v.at[i], p_sem.at[i])

    def c_load(i):
        at = pl.ds(i * CHUNK, CHUNK)
        return pltpu.make_async_copy(c_hbm.at[at], c_v.at[i], c_sem.at[i])

    def o_store(i):
        return pltpu.make_async_copy(o_v.at[i], o_hbm.at[pl.ds(i * CHUNK, CHUNK)], o_sem)

    def remote(source, target_ref, send, receive, device):
        return pltpu.make_async_remote_copy(
            src_ref=source, dst_ref=target_ref, send_sem=send, recv_sem=receive,
            device_id=device, device_id_type=MESH,
        )

    def far_down(i):
        return remote(far_s.at[i, 0], far_r.at[i, 0], far_ss, far_rs.at[i, 0], down)

    def far_up(i):
        return remote(far_s.at[i, 1], far_r.at[i, 1], far_ss, far_rs.at[i, 1], up)

    def near_down(i, source=None):
        source = lo_s.at[i] if source is None else source
        return remote(source, hi_r.at[i], lo_ss, hi_rs.at[i], down)

    def near_up(i, source=None):
        source = hi_s.at[i] if source is None else source
        return remote(source, lo_r.at[i], hi_ss, lo_rs.at[i], up)

    def move(i):
        at = i - EARLY
        return remote(move_s.at[at], move_r.at[at], move_ss, move_rs.at[at], across)

    def middle(i):
        return remote(mid_s.at[i], mid_r.at[i], mid_ss, mid_rs.at[i], across)

    pat_copies = [
        pltpu.make_async_copy(pp_hbm, p_pat, pat_sem.at[0]),
        pltpu.make_async_copy(sp_hbm, s_pat, pat_sem.at[1]),
    ]
    pat_copies[1].start()
    pat_copies[0].start()
    for k in range(4):
        s_load(k).start()
    p_load(0).start()
    for i in range(1, AHEAD + 1):
        p_load(i).start()

    def as_scale(value):
        return value.astype(jnp.float32).astype(jnp.bfloat16)

    pat_copies[1].wait()
    for k in range(4):
        s_load(k).wait()
        for b in range(8):
            rows, columns = pl.ds(b * BLOCK, BLOCK), pl.ds(k * BLOCK, BLOCK)
            keep = as_scale(s_pat[b, group * 4 + lax.rem(rep + k, 4)])
            s_v[rows, columns] = s_v[rows, columns] * keep
    pat_copies[0].wait()

    def product(i):
        p_load(i).wait()
        for a in range(CHUNK // BLOCK):
            for b in range(8):
                rows, columns = pl.ds(a * BLOCK, BLOCK), pl.ds(b * BLOCK, BLOCK)
                keep = as_scale(p_pat[b, i * (CHUNK // BLOCK) + a])
                p_v[i, rows, columns] = p_v[i, rows, columns] * keep
        return jnp.dot(p_v[i], s_v[...], preferred_element_type=jnp.float32)

    def share(i, term):
        far = term[:, 2 * BLOCK:3 * BLOCK].astype(jnp.bfloat16)
        far_s[i, 0] = far[:HALF]
        far_s[i, 1] = far[HALF:]
        far_down(i).start()
        far_up(i).start()
        own[i] = term[:, :BLOCK].astype(jnp.float32)
        hi_s[i, :HALF] = term[:HALF, BLOCK:2 * BLOCK].astype(jnp.bfloat16)
        wait_hi[i] = term[HALF:, BLOCK:2 * BLOCK].astype(jnp.float32)
        wait_lo[i] = term[:HALF, 3 * BLOCK:].astype(jnp.float32)
        lo_s[i, HALF:] = term[HALF:, 3 * BLOCK:].astype(jnp.bfloat16)

    def add(i):
        c_load(i).start()
        far_down(i).wait_recv()
        lo_s[i, :HALF] = (wait_lo[i] + far_r[i, 0].astype(jnp.float32)).astype(jnp.bfloat16)

        @pl.when(i >= EARLY)
        def _():
            near_down(i).start()

        far_up(i).wait_recv()
        hi_s[i, HALF:] = (wait_hi[i] + far_r[i, 1].astype(jnp.float32)).astype(jnp.bfloat16)

        @pl.when(i >= EARLY)
        def _():
            near_up(i).start()

        def gather(to):
            to[i, 0] = lo_s[i]
            to[i, 1] = hi_s[i]
            to[i, 2] = own[i].astype(jnp.bfloat16)

        @pl.when(jnp.logical_and(i < EARLY, moves))
        def _():
            gather(mid_s)
            middle(i).start()

        @pl.when(jnp.logical_and(i < EARLY, stays))
        def _():
            gather(mid_r)

    def resume(i):
        @pl.when(moves)
        def _():
            middle(i).wait_recv()

        near_down(i, mid_r.at[i, 0]).start()
        near_up(i, mid_r.at[i, 1]).start()

    def put(i, value):
        c_load(i).wait()
        o_v[i] = c_v[i] + value
        o_store(i).start()

    def arrived(i):
        near_down(i).wait_recv()
        near_up(i).wait_recv()
        return hi_r[i].astype(jnp.float32) + lo_r[i].astype(jnp.float32)

    def total(i):
        summed = own[i] + arrived(i)

        @pl.when(moves)
        def _():
            move_s[i - EARLY] = summed.astype(jnp.bfloat16)
            move(i).start()

        @pl.when(stays)
        def _():
            put(i, summed)

    def total_early(i):
        put(i, mid_r[i, 2].astype(jnp.float32) + arrived(i))

    def finish(i):
        move(i).wait_recv()
        put(i, move_r[i - EARLY].astype(jnp.float32))

    initial = product(0)

    @pl.when(moves)
    def _():
        pl.semaphore_wait(barrier, 4)

    @pl.when(stays)
    def _():
        pl.semaphore_wait(barrier, 2)

    share(0, initial)

    def within(value, low, high):
        return jnp.logical_and(value >= low, value < high)

    def body(t, carry):
        @pl.when(t + AHEAD < chunks)
        def _():
            p_load(t + AHEAD).start()

        @pl.when(t < chunks)
        def _():
            share(t, product(t))

        @pl.when(within(t, LAG_ADD, chunks + LAG_ADD))
        def _():
            add(t - LAG_ADD)

        @pl.when(within(t, chunks + LAG_ADD, chunks + EARLY + LAG_ADD))
        def _():
            resume(t - chunks - LAG_ADD)

        @pl.when(within(t, EARLY + LAG_SUM, chunks + LAG_SUM))
        def _():
            total(t - LAG_SUM)

        @pl.when(within(t, chunks + LAG_SUM, chunks + EARLY + LAG_SUM))
        def _():
            total_early(t - chunks - LAG_SUM)

        @pl.when(jnp.logical_and(moves, within(t, EARLY + LAG_OUT, chunks + LAG_OUT)))
        def _():
            finish(t - LAG_OUT)

        return carry

    lax.fori_loop(1, max(chunks + EARLY + LAG_SUM, chunks + LAG_OUT), body, 0)

    remote(far_s, far_r, far_ss, far_rs.at[0, 0], down).wait_send()
    remote(lo_s, hi_r, lo_ss, hi_rs.at[0], down).wait_send()
    remote(hi_s, lo_r, hi_ss, lo_rs.at[0], up).wait_send()

    @pl.when(moves)
    def _():
        remote(move_s, move_r, move_ss, move_rs.at[0], across).wait_send()
        remote(mid_s, mid_r, mid_ss, mid_rs.at[0], across).wait_send()

    pltpu.make_async_copy(o_hbm, o_hbm, o_sem).wait()


def cannon_step(shift, p_matrix, s_matrix, p_pattern, s_pattern, c_input):
    rows, depth = p_matrix.shape
    chunks = rows // CHUNK
    width = c_input.shape[1]
    plain = chunks - EARLY
    dma = pltpu.SemaphoreType.DMA
    half = lambda dtype, *lead: pltpu.VMEM((chunks, *lead, HALF, width), dtype)
    full = lambda dtype, count=chunks: pltpu.VMEM((count, CHUNK, width), dtype)
    early = pltpu.VMEM((EARLY, 3, CHUNK, width), jnp.bfloat16)
    return pl.pallas_call(
        functools.partial(kernel, shift, chunks),
        out_shape=jax.ShapeDtypeStruct(c_input.shape, jnp.float32),
        in_specs=[pl.BlockSpec(memory_space=pl.ANY)] * 5,
        out_specs=pl.BlockSpec(memory_space=pl.ANY),
        scratch_shapes=[
            pltpu.SMEM(p_pattern.shape, jnp.int32), pltpu.SMEM(s_pattern.shape, jnp.int32),
            pltpu.VMEM((chunks, CHUNK, depth), jnp.bfloat16),
            pltpu.VMEM((depth, 4 * width), jnp.bfloat16),
            full(jnp.float32), full(jnp.float32), full(jnp.float32),
            half(jnp.float32), half(jnp.float32),
            half(jnp.bfloat16, 2),
            full(jnp.bfloat16), full(jnp.bfloat16), full(jnp.bfloat16, plain), early,
            half(jnp.bfloat16, 2),
            full(jnp.bfloat16), full(jnp.bfloat16), full(jnp.bfloat16, plain), early,
            dma((2,)), dma((chunks,)), dma((4,)), dma((chunks,)), dma,
            dma, dma((chunks, 2)),
            dma, dma((chunks,)), dma, dma((chunks,)),
            dma, dma((plain,)), dma, dma((EARLY,)),
        ],
        compiler_params=pltpu.CompilerParams(
            collective_id=shift, has_side_effects=True, vmem_limit_bytes=56 * 2**20
        ),
        cost_estimate=pl.CostEstimate(
            flops=2 * rows * depth * 4 * width, bytes_accessed=20 * 2**20, transcendentals=0
        ),
    )(p_pattern, s_pattern, p_matrix, s_matrix, c_input)


def local(p_matrix, s_matrix, p_pattern, s_pattern, c_input, step):
    return lax.switch(
        lax.rem(step[0], 4),
        [functools.partial(cannon_step, shift) for shift in range(4)],
        p_matrix, s_matrix, p_pattern.T, s_pattern, c_input,
    )


def solution(mesh):
    placed = (
        P("row", ("col", "rep")),
        P(("col", "rep"), None),
        P("row", ("col", "rep")),
        P(("col", "rep"), None),
        P("row", ("col", "rep")),
        P(),
    )
    return jax.shard_map(
        local, mesh=mesh, in_specs=placed, out_specs=P("row", ("col", "rep")), check_vma=False
    )
```

time: 70 us -> 62.2 us (0.89)
  the two profiles are of different devices: /device:TPU:96 before, /device:TPU:1 now
where the time goes in v2:
time: 62.2 us; the launch traced here: 61.5 us
  Pallas kernels  59.1 us (95%)
  local copies, waits for them, and re-layouts  1.67 us (3%)
  between operations  0.67 us (1%)
    pallas_call x1, Pallas kernels, cannon_step(): pl.pallas_call(functools.partial(kernel, shift, chunks), out_shape=jax.Sh...  59.1 us
    unnamed x1, local copies, waits for them, and re-layouts  1.67 us

profile of v2, /device:TPU:1, one launch (start us, length us, event | category | flops | bytes accessed | tf_op | source)
XLA Modules:
  0.0 61.5 jit_solution(6559734129964505310)
XLA Ops:
  0.7 59.1 %conditional.1 = (f32[6144,128]{1,0:T(8,128)S(1)}) conditional(s32[]{:T(128)} %clamp.3, (s32[8,48]{1,0:T(8,128)}, s32[8,16]{1,0:T(8,128)}, bf16[6144,1024]{1,0:T(8,128)(2,1)}, bf16[1024,2048]{1,0:T(8,128)(2,1)}, f32[6144,128]{1,0:T(8,128)}) %tuple.26, (s32[8,48]{1,0:T(8,128)}, s32[8,16]{1,0:T(8,128)}, ...), branch_computations={%region_0.0_spmd, %region_1.0_spmd, %region_2.0_spmd, %region_3.0_... | conditional | flops 6442450944 | bytes 20971528 | solution.py:298
  0.7 59.1 %branch_2_fun.1 = f32[6144,128]{1,0:T(8,128)S(1)} custom-call(s32[8,48]{1,0:T(8,128)} %get-tuple-element.60.pp_hbm, s32[8,16]{1,0:T(8,128)} %get-tuple-element.89.sp_hbm, bf16[6144,1024]{1,0:T(8,128)(2,1)} %get-tuple-element.93.p_hbm, bf16[1024,2048]{1,0:T(8,128)(2,1)} %get-tuple-element.97.s_hbm, f32[6144,128]{1,0:T(8,128)} %get-tuple-element.101.c_hbm), custom_call_target="tpu_custom_call" | custom-call | flops 6442450944 | bytes 20971520 | tf_op jit(solution)/shard_map/cond/branch_2_fun/pallas_call | solution.py:268
  59.8 1.7 %copy.33 = f32[6144,128]{1,0:T(8,128)} copy(f32[6144,128]{1,0:T(8,128)S(1)} %get-tuple-element.70) | data formatting | bytes 6291456

commit v3 on v2

--- a/solution.py
+++ b/solution.py
@@ -11,8 +11,8 @@
 CHUNK = 512
 HALF = CHUNK // 2
 EARLY = 2
-AHEAD = 2
-LAG_ADD, LAG_SUM, LAG_OUT = 2, 4, 6
+AHEAD = 1
+LAG_ADD, LAG_SUM, LAG_OUT = 3, 5, 7
 MESH = pl.DeviceIdType.MESH
 
 
@@ -296,7 +296,7 @@
 
 def local(p_matrix, s_matrix, p_pattern, s_pattern, c_input, step):
     return lax.switch(
-        lax.rem(step[0], 4),
+        step[0] & 3,
         [functools.partial(cannon_step, shift) for shift in range(4)],
         p_matrix, s_matrix, p_pattern.T, s_pattern, c_input,
     )

time: 62.2 us -> 62.4 us (level)
  Pallas kernels: 59.1 us -> 59.8 us
    pallas_call x1, Pallas kernels: 59.1 us -> 59.8 us  [cannon_step(): pl.pallas_call(functools.partial(kernel, shift, chunks), out_shape=jax.Sh...]
where the time goes in v3:
time: 62.4 us; the launch traced here: 62.2 us
  Pallas kernels  59.8 us (96%)
  local copies, waits for them, and re-layouts  1.67 us (3%)
  between operations  0.66 us (1%)
    pallas_call x1, Pallas kernels, cannon_step(): pl.pallas_call(functools.partial(kernel, shift, chunks), out_shape=jax.Sh...  59.8 us
    unnamed x1, local copies, waits for them, and re-layouts  1.67 us

profile of v3, /device:TPU:1, one launch (start us, length us, event | category | flops | bytes accessed | tf_op | source)
XLA Modules:
  0.0 62.2 jit_solution(332236328596648691)
XLA Ops:
  0.7 59.8 %conditional.1 = (f32[6144,128]{1,0:T(8,128)S(1)}) conditional(s32[]{:T(128)} %bitcast, (s32[8,48]{1,0:T(8,128)}, s32[8,16]{1,0:T(8,128)}, bf16[6144,1024]{1,0:T(8,128)(2,1)}, bf16[1024,2048]{1,0:T(8,128)(2,1)}, f32[6144,128]{1,0:T(8,128)}) %tuple.26, (s32[8,48]{1,0:T(8,128)}, s32[8,16]{1,0:T(8,128)}, ...), branch_computations={%region_0.0_spmd, %region_1.0_spmd, %region_2.0_spmd, %region_3.0_... | conditional | flops 6442450944 | bytes 20971528 | solution.py:298
  0.7 59.8 %branch_1_fun.1 = f32[6144,128]{1,0:T(8,128)S(1)} custom-call(s32[8,48]{1,0:T(8,128)} %get-tuple-element.55.pp_hbm, s32[8,16]{1,0:T(8,128)} %get-tuple-element.88.sp_hbm, bf16[6144,1024]{1,0:T(8,128)(2,1)} %get-tuple-element.92.p_hbm, bf16[1024,2048]{1,0:T(8,128)(2,1)} %get-tuple-element.96.s_hbm, f32[6144,128]{1,0:T(8,128)} %get-tuple-element.100.c_hbm), custom_call_target="tpu_custom_call" | custom-call | flops 6442450944 | bytes 20971520 | tf_op jit(solution)/shard_map/cond/branch_1_fun/pallas_call | solution.py:268
  60.5 1.7 %copy.33 = f32[6144,128]{1,0:T(8,128)} copy(f32[6144,128]{1,0:T(8,128)S(1)} %get-tuple-element.70) | data formatting | bytes 6291456

commit v4 on v3

--- a/solution.py
+++ b/solution.py
@@ -12,6 +12,8 @@
 HALF = CHUNK // 2
 EARLY = 2
 AHEAD = 1
+SLOTS = (0, 1, 3, 2)
+HEAD = 2
 LAG_ADD, LAG_SUM, LAG_OUT = 3, 5, 7
 MESH = pl.DeviceIdType.MESH
 
@@ -41,14 +43,21 @@
         pl.semaphore_signal(barrier, inc=1, device_id=across, device_id_type=MESH)
         pl.semaphore_signal(barrier, inc=1, device_id={"col": origin}, device_id_type=MESH)
 
+    def s_block(k):
+        return group * 4 + lax.rem(rep + SLOTS[k], 4)
+
     def s_load(k):
-        at = pl.multiple_of((group * 4 + lax.rem(rep + k, 4)) * BLOCK, BLOCK)
+        at = pl.multiple_of(s_block(k) * BLOCK, BLOCK)
         return pltpu.make_async_copy(
             s_hbm.at[:, pl.ds(at, BLOCK)], s_v.at[:, pl.ds(k * BLOCK, BLOCK)], s_sem.at[k]
         )
 
     def p_load(i):
         return pltpu.make_async_copy(p_hbm.at[pl.ds(i * CHUNK, CHUNK)], p_v.at[i], p_sem.at[i])
+
+    def p_first(half):
+        at = pl.ds(half * HALF, HALF)
+        return pltpu.make_async_copy(p_hbm.at[at], p_v.at[0, at], p_sem.at[half * chunks])
 
     def c_load(i):
         at = pl.ds(i * CHUNK, CHUNK)
@@ -90,44 +99,56 @@
     ]
     pat_copies[1].start()
     pat_copies[0].start()
-    for k in range(4):
+    s_load(3).start()
+    p_first(0).start()
+    p_first(1).start()
+    p_load(1).start()
+    for k in range(3):
         s_load(k).start()
-    p_load(0).start()
-    for i in range(1, AHEAD + 1):
+    for i in range(2, HEAD + AHEAD):
         p_load(i).start()
 
     def as_scale(value):
         return value.astype(jnp.float32).astype(jnp.bfloat16)
 
-    pat_copies[1].wait()
-    for k in range(4):
+    def mask_s(k):
         s_load(k).wait()
         for b in range(8):
             rows, columns = pl.ds(b * BLOCK, BLOCK), pl.ds(k * BLOCK, BLOCK)
-            keep = as_scale(s_pat[b, group * 4 + lax.rem(rep + k, 4)])
-            s_v[rows, columns] = s_v[rows, columns] * keep
-    pat_copies[0].wait()
-
-    def product(i):
-        p_load(i).wait()
-        for a in range(CHUNK // BLOCK):
+            s_v[rows, columns] = s_v[rows, columns] * as_scale(s_pat[b, s_block(k)])
+
+    def mask_p(i, low, high):
+        for a in range(low, high):
             for b in range(8):
                 rows, columns = pl.ds(a * BLOCK, BLOCK), pl.ds(b * BLOCK, BLOCK)
                 keep = as_scale(p_pat[b, i * (CHUNK // BLOCK) + a])
                 p_v[i, rows, columns] = p_v[i, rows, columns] * keep
-        return jnp.dot(p_v[i], s_v[...], preferred_element_type=jnp.float32)
-
-    def share(i, term):
-        far = term[:, 2 * BLOCK:3 * BLOCK].astype(jnp.bfloat16)
+
+    def send_far(i):
+        far_down(i).start()
+        far_up(i).start()
+
+    def far_part(i, half):
+        left = p_v[i, pl.ds(half * HALF, HALF)]
+        far = jnp.dot(left, s_v[:, 3 * BLOCK:], preferred_element_type=jnp.float32)
+        far_s[i, half] = far.astype(jnp.bfloat16)
+
+    def keep_near(i, term):
+        own[i] = term[:, :BLOCK]
+        hi_s[i, :HALF] = term[:HALF, BLOCK:2 * BLOCK].astype(jnp.bfloat16)
+        wait_hi[i] = term[HALF:, BLOCK:2 * BLOCK]
+        wait_lo[i] = term[:HALF, 2 * BLOCK:3 * BLOCK]
+        lo_s[i, HALF:] = term[HALF:, 2 * BLOCK:3 * BLOCK].astype(jnp.bfloat16)
+
+    def produce(i):
+        p_load(i).wait()
+        mask_p(i, 0, CHUNK // BLOCK)
+        term = jnp.dot(p_v[i], s_v[...], preferred_element_type=jnp.float32)
+        far = term[:, 3 * BLOCK:].astype(jnp.bfloat16)
         far_s[i, 0] = far[:HALF]
         far_s[i, 1] = far[HALF:]
-        far_down(i).start()
-        far_up(i).start()
-        own[i] = term[:, :BLOCK].astype(jnp.float32)
-        hi_s[i, :HALF] = term[:HALF, BLOCK:2 * BLOCK].astype(jnp.bfloat16)
-        wait_hi[i] = term[HALF:, BLOCK:2 * BLOCK].astype(jnp.float32)
-        wait_lo[i] = term[:HALF, 3 * BLOCK:].astype(jnp.float32)
-        lo_s[i, HALF:] = term[HALF:, 3 * BLOCK:].astype(jnp.bfloat16)
+        send_far(i)
+        keep_near(i, term)
 
     def add(i):
         c_load(i).start()
@@ -196,7 +217,13 @@
         move(i).wait_recv()
         put(i, move_r[i - EARLY].astype(jnp.float32))
 
-    initial = product(0)
+    pat_copies[1].wait()
+    mask_s(3)
+    pat_copies[0].wait()
+    for half in range(2):
+        p_first(half).wait()
+        mask_p(0, half * HALF // BLOCK, (half + 1) * HALF // BLOCK)
+        far_part(0, half)
 
     @pl.when(moves)
     def _():
@@ -206,7 +233,17 @@
     def _():
         pl.semaphore_wait(barrier, 2)
 
-    share(0, initial)
+    send_far(0)
+    for i in range(1, HEAD):
+        p_load(i).wait()
+        mask_p(i, 0, CHUNK // BLOCK)
+        far_part(i, 0)
+        far_part(i, 1)
+        send_far(i)
+    for k in range(3):
+        mask_s(k)
+    for i in range(HEAD):
+        keep_near(i, jnp.dot(p_v[i], s_v[:, :3 * BLOCK], preferred_element_type=jnp.float32))
 
     def within(value, low, high):
         return jnp.logical_and(value >= low, value < high)
@@ -218,7 +255,7 @@
 
         @pl.when(t < chunks)
         def _():
-            share(t, product(t))
+            produce(t)
 
         @pl.when(within(t, LAG_ADD, chunks + LAG_ADD))
         def _():
@@ -242,7 +279,7 @@
 
         return carry
 
-    lax.fori_loop(1, max(chunks + EARLY + LAG_SUM, chunks + LAG_OUT), body, 0)
+    lax.fori_loop(HEAD, max(chunks + EARLY + LAG_SUM, chunks + LAG_OUT), body, 0)
 
     remote(far_s, far_r, far_ss, far_rs.at[0, 0], down).wait_send()
     remote(lo_s, hi_r, lo_ss, hi_rs.at[0], down).wait_send()
@@ -280,7 +317,7 @@
             full(jnp.bfloat16), full(jnp.bfloat16), full(jnp.bfloat16, plain), early,
             half(jnp.bfloat16, 2),
             full(jnp.bfloat16), full(jnp.bfloat16), full(jnp.bfloat16, plain), early,
-            dma((2,)), dma((chunks,)), dma((4,)), dma((chunks,)), dma,
+            dma((2,)), dma((chunks + 1,)), dma((4,)), dma((chunks,)), dma,
             dma, dma((chunks, 2)),
             dma, dma((chunks,)), dma, dma((chunks,)),
             dma, dma((plain,)), dma, dma((EARLY,)),

time: 62.4 us -> 61.7 us (0.989)
  Pallas kernels: 59.8 us -> 58.9 us
    pallas_call x1, Pallas kernels: 59.8 us -> 58.9 us  [cannon_step(): pl.pallas_call(functools.partial(kernel, shift, chunks), out_shape=jax.Sh...]
where the time goes in v4:
time: 61.7 us; the launch traced here: 61.5 us
  Pallas kernels  58.9 us (95%)
  local copies, waits for them, and re-layouts  1.67 us (3%)
  between operations  0.66 us (1%)
    pallas_call x1, Pallas kernels, cannon_step(): pl.pallas_call(functools.partial(kernel, shift, chunks), out_shape=jax.Sh...  58.9 us
    unnamed x1, local copies, waits for them, and re-layouts  1.67 us

profile of v4, /device:TPU:1, one launch (start us, length us, event | category | flops | bytes accessed | tf_op | source)
XLA Modules:
  0.0 61.5 jit_solution(13400302273094478460)
XLA Ops:
  0.7 59.1 %conditional.1 = (f32[6144,128]{1,0:T(8,128)S(1)}) conditional(s32[]{:T(128)} %bitcast, (s32[8,48]{1,0:T(8,128)}, s32[8,16]{1,0:T(8,128)}, bf16[6144,1024]{1,0:T(8,128)(2,1)}, bf16[1024,2048]{1,0:T(8,128)(2,1)}, f32[6144,128]{1,0:T(8,128)}) %tuple.26, (s32[8,48]{1,0:T(8,128)}, s32[8,16]{1,0:T(8,128)}, ...), branch_computations={%region_0.0_spmd, %region_1.0_spmd, %region_2.0_spmd, %region_3.0_... | conditional | flops 6442450944 | bytes 20971528 | solution.py:335
  0.7 58.9 %branch_2_fun.1 = f32[6144,128]{1,0:T(8,128)S(1)} custom-call(s32[8,48]{1,0:T(8,128)} %get-tuple-element.60.pp_hbm, s32[8,16]{1,0:T(8,128)} %get-tuple-element.89.sp_hbm, bf16[6144,1024]{1,0:T(8,128)(2,1)} %get-tuple-element.93.p_hbm, bf16[1024,2048]{1,0:T(8,128)(2,1)} %get-tuple-element.97.s_hbm, f32[6144,128]{1,0:T(8,128)} %get-tuple-element.101.c_hbm), custom_call_target="tpu_custom_call" | custom-call | flops 6442450944 | bytes 20971520 | tf_op jit(solution)/shard_map/cond/branch_2_fun/pallas_call | solution.py:305
  59.8 1.7 %copy.33 = f32[6144,128]{1,0:T(8,128)} copy(f32[6144,128]{1,0:T(8,128)S(1)} %get-tuple-element.70) | data formatting | bytes 6291456

commit v5 on v3

--- a/solution.py
+++ b/solution.py
@@ -69,13 +69,19 @@
     def far_up(i):
         return remote(far_s.at[i, 1], far_r.at[i, 1], far_ss, far_rs.at[i, 1], up)
 
-    def near_down(i, source=None):
-        source = lo_s.at[i] if source is None else source
-        return remote(source, hi_r.at[i], lo_ss, hi_rs.at[i], down)
-
-    def near_up(i, source=None):
-        source = hi_s.at[i] if source is None else source
-        return remote(source, lo_r.at[i], hi_ss, lo_rs.at[i], up)
+    def near_down(i):
+        return remote(lo_s.at[i], hi_r.at[i], lo_ss, hi_rs.at[i], down)
+
+    def near_up(i):
+        return remote(hi_s.at[i], lo_r.at[i], hi_ss, lo_rs.at[i], up)
+
+    def end_down(i, half):
+        at = pl.ds(half * HALF, HALF)
+        return remote(mid_r.at[i, 0, at], hi_r.at[i, at], lo_ss, hi_rs.at[chunks + 2 * i + half], down)
+
+    def end_up(i, half):
+        at = pl.ds(half * HALF, HALF)
+        return remote(mid_r.at[i, 1, at], lo_r.at[i, at], hi_ss, lo_rs.at[chunks + 2 * i + half], up)
 
     def move(i):
         at = i - EARLY
@@ -164,8 +170,9 @@
         def _():
             middle(i).wait_recv()
 
-        near_down(i, mid_r.at[i, 0]).start()
-        near_up(i, mid_r.at[i, 1]).start()
+        for half in range(2):
+            end_down(i, half).start()
+            end_up(i, half).start()
 
     def put(i, value):
         c_load(i).wait()
@@ -190,7 +197,16 @@
             put(i, summed)
 
     def total_early(i):
-        put(i, mid_r[i, 2].astype(jnp.float32) + arrived(i))
+        c_load(i).wait()
+        for half in range(2):
+            at = pl.ds(half * HALF, HALF)
+            end_down(i, half).wait_recv()
+            end_up(i, half).wait_recv()
+            both = hi_r[i, at].astype(jnp.float32) + lo_r[i, at].astype(jnp.float32)
+            o_v[i, at] = c_v[i, at] + (mid_r[i, 2, at].astype(jnp.float32) + both)
+            pltpu.make_async_copy(
+                o_v.at[i, at], o_hbm.at[pl.ds(i * CHUNK + half * HALF, HALF)], o_sem
+            ).start()
 
     def finish(i):
         move(i).wait_recv()
@@ -282,7 +298,7 @@
             full(jnp.bfloat16), full(jnp.bfloat16), full(jnp.bfloat16, plain), early,
             dma((2,)), dma((chunks,)), dma((4,)), dma((chunks,)), dma,
             dma, dma((chunks, 2)),
-            dma, dma((chunks,)), dma, dma((chunks,)),
+            dma, dma((chunks + 2 * EARLY,)), dma, dma((chunks + 2 * EARLY,)),
             dma, dma((plain,)), dma, dma((EARLY,)),
         ],
         compiler_params=pltpu.CompilerParams(

time: 62.4 us -> 61.7 us (0.989); the launches traced: 62.2 us -> 60.6 us
  Pallas kernels: 59.8 us -> 58.3 us
    pallas_call x1, Pallas kernels: 59.8 us -> 58.3 us  [cannon_step(): pl.pallas_call(functools.partial(kernel, shift, chunks), out_shape=jax.Sh...]
where the time goes in v5:
time: 61.7 us; the launch traced here: 60.6 us
  Pallas kernels  58.3 us (94%)
  local copies, waits for them, and re-layouts  1.67 us (3%)
  between operations  0.66 us (1%)
    pallas_call x1, Pallas kernels, cannon_step(): pl.pallas_call(functools.partial(kernel, shift, chunks), out_shape=jax.Sh...  58.3 us
    unnamed x1, local copies, waits for them, and re-layouts  1.67 us

profile of v5, /device:TPU:1, one launch (start us, length us, event | category | flops | bytes accessed | tf_op | source)
XLA Modules:
  0.0 60.6 jit_solution(3156132416551809068)
XLA Ops:
  0.7 58.3 %conditional.1 = (f32[6144,128]{1,0:T(8,128)S(1)}) conditional(s32[]{:T(128)} %bitcast, (s32[8,48]{1,0:T(8,128)}, s32[8,16]{1,0:T(8,128)}, bf16[6144,1024]{1,0:T(8,128)(2,1)}, bf16[1024,2048]{1,0:T(8,128)(2,1)}, f32[6144,128]{1,0:T(8,128)}) %tuple.26, (s32[8,48]{1,0:T(8,128)}, s32[8,16]{1,0:T(8,128)}, ...), branch_computations={%region_0.0_spmd, %region_1.0_spmd, %region_2.0_spmd, %region_3.0_... | conditional | flops 6442450944 | bytes 20971528 | solution.py:314
  0.7 58.3 %branch_0_fun.1 = f32[6144,128]{1,0:T(8,128)S(1)} custom-call(s32[8,48]{1,0:T(8,128)} %get-tuple-element.48.pp_hbm, s32[8,16]{1,0:T(8,128)} %get-tuple-element.87.sp_hbm, bf16[6144,1024]{1,0:T(8,128)(2,1)} %get-tuple-element.91.p_hbm, bf16[1024,2048]{1,0:T(8,128)(2,1)} %get-tuple-element.95.s_hbm, f32[6144,128]{1,0:T(8,128)} %get-tuple-element.99.c_hbm), custom_call_target="tpu_custom_call" | custom-call | flops 6442450944 | bytes 20971520 | tf_op jit(solution)/shard_map/cond/branch_0_fun/pallas_call | solution.py:284
  59.0 1.7 %copy.33 = f32[6144,128]{1,0:T(8,128)} copy(f32[6144,128]{1,0:T(8,128)S(1)} %get-tuple-element.70) | data formatting | bytes 6291456
